TPU v7x, 32 devices: a whole 2x2x4 slice. The times are simulated.
32 devices in a mesh: expert: 4 (over y, core), hidden: 8 (over z, x).
Axes of the slice: x: 2, y: 2, z: 4, core: 2. Of those that a mesh axis runs over, the one named last changes fastest.
Arguments:
- tokens: bfloat16 [512, 3584], P('hidden'), may hold values from -6 to 6
- cotangent: bfloat16 [512, 3584], P('hidden'), may hold values from -6 to 6
- routes: int32 [512, 8], P('hidden'), may hold values from 0 to 63, all different within a row; in each aligned block of 64 rows (0 to 63, 64 to 127, ...) at most 20 rows name the same one
- route_weights: float32 [512, 8], P('hidden'), may hold values from 0.08 to 1
- gate_weight: bfloat16 [65536, 3584], P(('expert', 'hidden')), may hold values from -0.09375 to 0.09375
- up_weight: bfloat16 [65536, 3584], P(('expert', 'hidden')), may hold values from -0.09375 to 0.09375
- down_weight: bfloat16 [65536, 3584], P(('expert', 'hidden')), may hold values from -6 to 6
- cluster: int32 [64], replicated, may hold values from 0 to 23, as said below
- merged_slot: int32 [24], replicated, may hold values from 0 to 23, each once
Outputs:
- merged_down: bfloat16 [24, 1, 1024, 3584], P('expert', None, 'hidden')
Inputs may be any that keep to these rules, and one draw needn't show every extreme that they name: `routes`: each row names 8 different experts. Within the rows of one shard of 64 tokens no expert is named by more than 20 rows, a bound that some block reaches. Every one of the 24 clusters has 1 to 6 member experts, and some cluster has exactly 6. `merged_slot`: each slot holds exactly one cluster.
All inputs are finite; a program needn't handle non-finite values.
Results may differ from a plain program's by a relative error of at most 0.014.
Values may be sent and summed in bfloat16 or wider, within the bound.
A program may use at most 192 MiB of HBM per device.

v0:
```python
import jax
import jax.numpy as jnp
from jax import lax
from jax.sharding import PartitionSpec as P

F = 1024
EXPERTS = 64
MERGED = 24
CAP = 20


PRIOR = 0.1


def slot_lookup(cluster, merged_slot):
    merged_ids = jnp.arange(MERGED, dtype=jnp.int32)
    return jnp.sum(
        jnp.where(cluster[:, None] == merged_ids[None, :], merged_slot[None, :], 0), axis=1
    )


def pack_rows(tokens, cotangent, routes, route_weights, first_expert, group_size):
    tok_count = tokens.shape[0]
    members = first_expert + jnp.arange(group_size, dtype=jnp.int32)
    matches = routes[:, :, None] == members[None, None, :]
    marked = jnp.any(matches, axis=1).astype(jnp.int32)
    places = jnp.cumsum(marked, axis=0) - marked
    slot_weight = jnp.sum(jnp.where(matches, route_weights[:, :, None], 0.0), axis=1)
    places_all = jnp.arange(CAP, dtype=jnp.int32)
    chosen = (marked.T[:, None, :] == 1) & (places.T[:, None, :] == places_all[None, :, None])
    picker = chosen.astype(jnp.bfloat16).reshape(group_size * CAP, tok_count)
    token_rows = jnp.dot(picker, tokens, preferred_element_type=jnp.float32).astype(jnp.bfloat16)
    cot_rows = jnp.dot(picker, cotangent, preferred_element_type=jnp.float32)
    scales = jnp.sum(jnp.where(chosen, slot_weight.T[:, None, :], 0.0), axis=2).reshape(
        group_size * CAP, 1
    )
    grad_rows = (scales * cot_rows).astype(jnp.bfloat16)
    return (token_rows, grad_rows)


def spread(packed, group_size, copies, hidden_count, local_count):
    width = packed.shape[-1]
    packed = packed.reshape(group_size, 1, CAP, width)
    packed = jnp.broadcast_to(packed, (group_size, copies, CAP, width))
    return packed.reshape(hidden_count, local_count, CAP, width)


def activate(token_recv, gate_local, up_local):
    gate_value = jnp.einsum(
        "jicd,isd->jics", token_recv, gate_local, preferred_element_type=jnp.float32
    )
    up_value = jnp.einsum(
        "jicd,isd->jics", token_recv, up_local, preferred_element_type=jnp.float32
    )
    hidden_act = jax.nn.silu(gate_value) * up_value
    return (hidden_act * hidden_act).astype(jnp.bfloat16)


def slot_mixer(slot_range, first_expert, member_local, slice_ids, copies, slot_table):
    experts = first_expert + member_local
    expert_ids = jnp.arange(EXPERTS, dtype=jnp.int32)
    member_slots = jnp.sum(
        jnp.where(experts[:, :, None] == expert_ids[None, None, :], slot_table[None, None, :], 0),
        axis=2,
    )
    slice_range = jnp.arange(copies, dtype=jnp.int32)
    same_slot = member_slots[None, None, :, :] == slot_range[:, None, None, None]
    same_slice = slice_ids[None, None, :, :] == slice_range[None, :, None, None]
    return (same_slot & same_slice).astype(jnp.bfloat16)


def per_device(
    tokens,
    cotangent,
    routes,
    route_weights,
    gate_weight,
    up_weight,
    down_weight,
    cluster,
    merged_slot,
):
    hidden_count = lax.axis_size("hidden")
    expert_count = lax.axis_size("expert")
    expert_index = lax.axis_index("expert")
    rows_dev = gate_weight.shape[0]
    width = gate_weight.shape[1]
    local_count = max(1, rows_dev // F)
    slice_rows = min(rows_dev, F)
    copies = F // slice_rows
    group_size = EXPERTS // expert_count
    piece_rows = slice_rows // hidden_count
    first_expert = expert_index * group_size
    token_rows, grad_rows = pack_rows(
        tokens, cotangent, routes, route_weights, first_expert, group_size
    )
    token_send = spread(token_rows, group_size, copies, hidden_count, local_count)
    grad_send = spread(grad_rows, group_size, copies, hidden_count, local_count)
    gate_local = gate_weight.reshape(local_count, slice_rows, width)
    up_local = up_weight.reshape(local_count, slice_rows, width)
    token_recv, grad_recv = (
        lax.all_to_all(token_send, "hidden", split_axis=0, concat_axis=0, tiled=True),
        lax.all_to_all(grad_send, "hidden", split_axis=0, concat_axis=0, tiled=True),
    )
    hidden_sq = activate(token_recv, gate_local, up_local)
    grad_wide = grad_recv.astype(jnp.float32)
    grad_sq = (grad_wide * grad_wide).astype(jnp.bfloat16)
    fisher = jnp.einsum("jics,jicd->isd", hidden_sq, grad_sq, preferred_element_type=jnp.float32)
    weighting = fisher + PRIOR
    down_local = down_weight.reshape(local_count, slice_rows, width).astype(jnp.float32)
    numer = (
        (weighting * down_local)
        .astype(jnp.bfloat16)
        .reshape(local_count, hidden_count, piece_rows, width)
    )
    denom = weighting.astype(jnp.bfloat16).reshape(local_count, hidden_count, piece_rows, width)
    numer_recv, denom_recv = (
        lax.all_to_all(numer, "hidden", split_axis=1, concat_axis=1, tiled=True),
        lax.all_to_all(denom, "hidden", split_axis=1, concat_axis=1, tiled=True),
    )
    sources = jnp.arange(hidden_count, dtype=jnp.int32)[None, :]
    local_ids = jnp.arange(local_count, dtype=jnp.int32)[:, None]
    start_row = sources * rows_dev + local_ids * slice_rows
    member_local = start_row // F
    slice_ids = start_row % F // slice_rows
    slot_table = slot_lookup(cluster, merged_slot)
    mixer = slot_mixer(
        jnp.arange(MERGED, dtype=jnp.int32),
        first_expert,
        member_local,
        slice_ids,
        copies,
        slot_table,
    )
    numer_part = jnp.einsum(
        "msih,ihqd->msqd", mixer, numer_recv, preferred_element_type=jnp.float32
    )
    denom_part = jnp.einsum(
        "msih,ihqd->msqd", mixer, denom_recv, preferred_element_type=jnp.float32
    )
    numer_total, denom_total = (
        lax.psum_scatter(
            numer_part.astype(jnp.bfloat16), "expert", scatter_dimension=0, tiled=True
        ).astype(jnp.float32),
        lax.psum_scatter(
            denom_part.astype(jnp.bfloat16), "expert", scatter_dimension=0, tiled=True
        ).astype(jnp.float32),
    )
    return (numer_total / denom_total).astype(jnp.bfloat16)


def solution(mesh):
    return jax.shard_map(
        per_device,
        mesh=mesh,
        in_specs=(
            P("hidden", None),
            P("hidden", None),
            P("hidden", None),
            P("hidden", None),
            P(("expert", "hidden"), None),
            P(("expert", "hidden"), None),
            P(("expert", "hidden"), None),
            P(),
            P(),
        ),
        out_specs=P("expert", None, "hidden", None),
        check_vma=False,
    )
```

profile of v0, /device:TPU:0, one launch (start us, length us, event | category | flops | bytes accessed | tf_op | source)
XLA Modules:
  0.0 1120.9 jit_solution(8997174316970483757)
XLA Ops:
  6.5 0.8 compare_reduce_fusion
  7.4 0.1 copy.57
  7.5 0.8 fusion.24
  8.4 0.1 reduce_window_sum.11
  8.6 0.1 select_reduce_fusion
  9.0 0.1 compare_and_fusion
  9.1 2.1 fusion.6
  11.2 2.6 reshape_reshape.7
  13.8 3.2 copy.63
  17.0 7.3 all-to-all-start.1
  24.2 2.1 convolution_convert_fusion
  26.3 2.6 reshape_reshape.6
  28.9 3.1 copy.60
  32.1 44.7 %all-to-all-done.1 = bf16[8,2,20,3584]{3,1,2,0:T(2,128)(2,1)} async-done(((bf16[8,2,20,3584]{3,1,2,0:T(2,128)(2,1)}), bf16[8,2,20,3584]{3,1,2,0:T(2,128)(2,1)}, u32[]{:S(2)}, u32[]{:S(2)}) %all-to-all-start.1) | async-done | bytes 2293792 | tf_op jit(solution)/shard_map/all_to_all | solution.py:103
  76.8 3.8 all-to-all-start
  80.6 3.7 multiply_convert_fusion
  84.3 48.8 %all-to-all-done = bf16[8,2,20,3584]{3,1,2,0:T(2,128)(2,1)S(1)} async-done(((bf16[8,2,20,3584]{3,1,2,0:T(2,128)(2,1)}), bf16[8,2,20,3584]{3,1,2,0:T(2,128)(2,1)S(1)}, u32[]{:S(2)}, u32[]{:S(2)}) %all-to-all-start) | async-done | bytes 2293792 | tf_op jit(solution)/shard_map/all_to_all | solution.py:102
  133.1 11.3 %fusion.11 = f32[2,8,20,1024]{3,2,1,0:T(8,128)} fusion(bf16[2,1024,3584,1]{2,1,3,0:T(8,128)(2,1)} %bitcast.80, bf16[8,2,20,3584]{3,1,2,0:T(2,128)(2,1)S(1)} %all-to-all-done), kind=kOutput, calls=%fused_computation.19 | convolution fusion | flops 2348810240 | bytes 18284544 | tf_op jit(solution)/shard_map/jicd,isd->jics/dot_general | solution.py:49
  144.4 25.3 %fusion = (bf16[2,1024,3584]{2,1,0:T(8,128)(2,1)}, bf16[2,1024,3584]{2,1,0:T(8,128)(2,1)}) fusion(bf16[2,1024,3584]{2,1,0:T(8,128)(2,1)} %bitcast.81, bf16[8,2,20,3584]{3,0,2,1:T(8,128)(2,1)} %multiply_convert_fusion, f32[2,8,20,1024]{3,2,1,0:T(8,128)} %fusion.11, bf16[2,1024,3584,1]{2,1,3,0:T(8,128)(2,1)} %bitcast.82, ...), kind=kOutput, calls=%fused_computation.3 | convolution fusion | flops 4736614400 | bytes 64618496 | tf_op jit(solution)/shard_map/jics,jicd->isd/dot_general | solution.py:108
  169.7 27.5 %copy.66 = bf16[2,8,128,3584]{3,0,2,1:T(2,128)(2,1)} copy(bf16[2,8,128,3584]{3,2,1,0:T(8,128)(2,1)} %bitcast.78) | data formatting | bytes 29360128 | tf_op jit(solution)/shard_map/reshape | solution.py:114
  197.1 5.7 all-to-all-start.2
  203.1 0.2 select_reduce_fusion.2
  203.4 316.7 %all-to-all-done.2 = bf16[2,8,128,3584]{3,0,2,1:T(2,128)(2,1)} async-done(((bf16[2,8,128,3584]{3,0,2,1:T(2,128)(2,1)}), bf16[2,8,128,3584]{3,0,2,1:T(2,128)(2,1)}, u32[]{:S(2)}, u32[]{:S(2)}) %all-to-all-start.2) | async-done | bytes 14680096 | tf_op jit(solution)/shard_map/all_to_all | solution.py:118
  520.0 15.7 %fusion.2 = bf16[24,1,128,3584]{3,0,2,1:T(8,128)(2,1)} fusion(bf16[2,8,128,3584]{3,0,2,1:T(2,128)(2,1)} %all-to-all-done.2, s32[2,8]{1,0:T(2,128)S(1)} %select_reduce_fusion.2, pred[2,8]{1,0:T(4,128)(4,1)S(1)} %fusion.34), kind=kOutput, calls=%fused_computation.6 | convolution fusion | flops 363332352 | bytes 36700240 | tf_op jit(solution)/shard_map/msih,ihqd->msqd/dot_general | solution.py:135
  535.8 23.2 %copy.68 = bf16[24,1,128,3584]{3,2,1,0:T(8,128)(2,1)} copy(bf16[24,1,128,3584]{3,0,2,1:T(8,128)(2,1)} %fusion.2) | data formatting | bytes 44040192 | tf_op jit(solution)/shard_map/convert_element_type | solution.py:143
  559.0 0.3 reduce-scatter.5.cloned.1.call-start
  559.3 26.6 %copy.69 = bf16[2,8,128,3584]{3,0,2,1:T(2,128)(2,1)S(1)} copy(bf16[2,8,128,3584]{3,2,1,0:T(8,128)(2,1)} %bitcast.77) | data formatting | bytes 29360128 | tf_op jit(solution)/shard_map/reshape | solution.py:116
  585.9 321.6 %all_to_all.20 = bf16[2,8,128,3584]{3,0,2,1:T(2,128)(2,1)} all-to-all(bf16[2,8,128,3584]{3,0,2,1:T(2,128)(2,1)S(1)} %copy.69), channel_id=1, replica_groups=mesh['expert'=4,'hidden'=8] {'hidden'}, dimensions={1} | all-to-all | bytes 29360128 | tf_op jit(solution)/shard_map/all_to_all | solution.py:119
  907.5 15.7 %fusion.3 = bf16[24,1,128,3584]{3,0,2,1:T(8,128)(2,1)} fusion(bf16[2,8,128,3584]{3,0,2,1:T(2,128)(2,1)} %all_to_all.20, s32[2,8]{1,0:T(2,128)S(1)} %select_reduce_fusion.2, pred[2,8]{1,0:T(4,128)(4,1)S(1)} %fusion.34), kind=kOutput, calls=%fused_computation.7 | convolution fusion | flops 363332352 | bytes 36700240 | tf_op jit(solution)/shard_map/msih,ihqd->msqd/dot_general | solution.py:138
  923.2 23.2 %copy.71 = bf16[24,1,128,3584]{3,2,1,0:T(8,128)(2,1)} copy(bf16[24,1,128,3584]{3,0,2,1:T(8,128)(2,1)} %fusion.3) | data formatting | bytes 44040192 | tf_op jit(solution)/shard_map/convert_element_type | solution.py:146
  946.5 159.1 %reduce-scatter.5.cloned.1.call-done = bf16[6,1,128,3584]{3,2,1,0:T(8,128)(2,1)} async-done(((bf16[24,1,128,3584]{3,2,1,0:T(8,128)(2,1)}), bf16[6,1,128,3584]{3,2,1,0:T(8,128)(2,1)}) %reduce-scatter.5.cloned.1.call-update) | async-done | bytes 5505040 | tf_op jit(solution)/shard_map/reduce_scatter | solution.py:145
  1105.6 8.5 divide_convert_fusion
  (31 shorter events, 0.8 us)
Async XLA Ops:
  6.5 2.6 copy-start
  13.8 10.4 copy-start.2
  17.0 59.8 %all-to-all-start.1 = ((bf16[8,2,20,3584]{3,1,2,0:T(2,128)(2,1)}), bf16[8,2,20,3584]{3,1,2,0:T(2,128)(2,1)}, u32[]{:S(2)}, u32[]{:S(2)}) async-start(bf16[8,2,20,3584]{3,1,2,0:T(2,128)(2,1)} %copy.63), calls=%async_computation.1 | async-start | bytes 4587520 | tf_op jit(solution)/shard_map/all_to_all | solution.py:103
  76.8 56.3 %all-to-all-start = ((bf16[8,2,20,3584]{3,1,2,0:T(2,128)(2,1)}), bf16[8,2,20,3584]{3,1,2,0:T(2,128)(2,1)S(1)}, u32[]{:S(2)}, u32[]{:S(2)}) async-start(bf16[8,2,20,3584]{3,1,2,0:T(2,128)(2,1)} %copy.60), calls=%async_computation | async-start | bytes 4587520 | tf_op jit(solution)/shard_map/all_to_all | solution.py:102
  197.1 5.8 copy-start.3
  197.1 5.8 copy-start.4
  197.1 322.9 %all-to-all-start.2 = ((bf16[2,8,128,3584]{3,0,2,1:T(2,128)(2,1)}), bf16[2,8,128,3584]{3,0,2,1:T(2,128)(2,1)}, u32[]{:S(2)}, u32[]{:S(2)}) async-start(bf16[2,8,128,3584]{3,0,2,1:T(2,128)(2,1)} %copy.66), calls=%async_computation.2 | async-start | bytes 29360128 | tf_op jit(solution)/shard_map/all_to_all | solution.py:118
  202.8 743.7 %reduce-scatter.3.cloned.1.call-start = ((), (), s32[]{:S(2)}) async-start(), calls=%async_computation.6 | async-start | bytes 27525120 | tf_op jit(solution)/shard_map/reduce_scatter | solution.py:142
  559.0 546.6 %reduce-scatter.5.cloned.1.call-start = ((), (), s32[]{:S(2)}) async-start(), calls=%async_computation.7 | async-start | bytes 27525120 | tf_op jit(solution)/shard_map/reduce_scatter | solution.py:145
  946.5 167.6 %copy-start.1 = (bf16[64,3584]{1,0:T(8,128)(2,1)S(1)}, bf16[64,3584]{1,0:T(8,128)(2,1)}, u32[]{:S(2)}) copy-start(bf16[64,3584]{1,0:T(8,128)(2,1)} %param.10) | copy-start | bytes 1376260
Sparse Core Ops, SparseCore 0:
  559.1 158.9 reduce-scatter.2
  946.6 158.9 reduce-scatter.4
where the time goes:
time: 1120 us
  waiting for transfers between devices  569 us (51%)
  blocking collectives  322 us (29%)
  local copies, waits for them, and re-layouts  113 us (10%)
  matrix products  72.2 us (6%)
  starting transfers between devices  17 us (2%)
  other arithmetic  14.6 us (1%)
  between operations  13.6 us (1%)
    all_to_all x1, blocking collectives, per_device(): lax.all_to_all(denom, 'hidden', split_axis=1, concat_axis=1, tiled=True)  322 us
    all_to_all x1, waiting for transfers between devices, per_device(): lax.all_to_all(numer, 'hidden', split_axis=1, concat_axis=1, tiled=True)  317 us
    reduce_scatter x1, waiting for transfers between devices, per_device(): lax.psum_scatter(denom_part.astype(jnp.bfloat16), 'expert', scatter_dimen...  159 us
    all_to_all x1, waiting for transfers between devices, per_device(): lax.all_to_all(token_send, 'hidden', split_axis=0, concat_axis=0, tiled=T...  48.8 us
    all_to_all x1, waiting for transfers between devices, per_device(): lax.all_to_all(grad_send, 'hidden', split_axis=0, concat_axis=0, tiled=True)  44.7 us
    reshape x1, local copies, waits for them, and re-layouts, per_device(): numer = (weighting * down_local).astype(jnp.bfloat16).reshape(local_count...  27.5 us
    reshape x1, local copies, waits for them, and re-layouts, per_device(): weighting.astype(jnp.bfloat16)  26.6 us
    dot_general x1, matrix products, per_device(): jnp.einsum('jics,jicd->isd', hidden_sq, grad_sq, preferred_element_type=j...  25.3 us
  transfers between devices with their start and end apart: 5, of which 4 were waited for; matrix products, arithmetic and copies ran while one was open for 7% of the time, Pallas kernels for 0%

commit v1 on v0

v1 whole, which is shorter than its diff:
```python
import jax
import jax.numpy as jnp
from jax import lax
from jax.experimental import pallas as pl
from jax.experimental.pallas import tpu as pltpu
from jax.sharding import PartitionSpec as P

F = 1024
EXPERTS = 64
MERGED = 24

PRIOR = 0.1


def slot_lookup(cluster, merged_slot):
    merged_ids = jnp.arange(MERGED, dtype=jnp.int32)
    return jnp.sum(
        jnp.where(cluster[:, None] == merged_ids[None, :], merged_slot[None, :], 0), axis=1
    )


def chunk_bounds(width):
    if width % (7 * 128):
        return [(0, width)]
    unit = width // 7
    cuts = [0, 2 * unit, 4 * unit, 6 * unit, 7 * unit]
    return list(zip(cuts[:-1], cuts[1:]))


def fold_kernel(slots_ref, act_ref, cot_ref, down_ref, out_ref, total):
    total[...] = jnp.zeros_like(total)
    for unit in range(act_ref.shape[0]):
        fisher = jnp.dot(act_ref[unit], cot_ref[...], preferred_element_type=jnp.float32)
        numer = (fisher + PRIOR) * down_ref[unit].astype(jnp.float32)
        slot = slots_ref[unit]
        total[slot] = total[slot] + numer
    out_ref[...] = total[...].astype(out_ref.dtype)


def fold(unit_slots, act, cot_sq, down, slot_count):
    units, piece, tok_count = act.shape
    width = down.shape[-1]
    block = 512 if width % 512 == 0 else (256 if width % 256 == 0 else 128)
    return pl.pallas_call(
        fold_kernel,
        grid_spec=pltpu.PrefetchScalarGridSpec(
            num_scalar_prefetch=1,
            grid=(width // block,),
            in_specs=[
                pl.BlockSpec((units, piece, tok_count), lambda i, s: (0, 0, 0)),
                pl.BlockSpec((tok_count, block), lambda i, s: (0, i)),
                pl.BlockSpec((units, piece, block), lambda i, s: (0, 0, i)),
            ],
            out_specs=pl.BlockSpec((slot_count, piece, block), lambda i, s: (0, 0, i)),
            scratch_shapes=[pltpu.VMEM((slot_count, piece, block), jnp.float32)],
        ),
        out_shape=jax.ShapeDtypeStruct((slot_count, piece, width), jnp.bfloat16),
        compiler_params=pltpu.CompilerParams(vmem_limit_bytes=40 * 1024 * 1024),
        cost_estimate=pl.CostEstimate(
            flops=2 * units * piece * tok_count * width,
            bytes_accessed=2 * (units + slot_count) * piece * width,
            transcendentals=0,
        ),
    )(unit_slots, act, cot_sq, down)


def per_device(
    tokens,
    cotangent,
    routes,
    route_weights,
    gate_weight,
    up_weight,
    down_weight,
    cluster,
    merged_slot,
):
    hidden_count = lax.axis_size("hidden")
    expert_count = lax.axis_size("expert")
    expert_index = lax.axis_index("expert")
    hidden_index = lax.axis_index("hidden")
    rows_dev, width = gate_weight.shape
    local_count = max(1, rows_dev // F)
    slice_rows = min(rows_dev, F)
    copies = F // slice_rows
    group_size = EXPERTS // expert_count
    piece = slice_rows // hidden_count
    first_expert = expert_index * group_size
    units = hidden_count * local_count
    slot_count = MERGED * copies
    own_slots = MERGED // expert_count
    top = routes.shape[1]

    down_view = down_weight.reshape(local_count, hidden_count, piece, width)
    bounds = chunk_bounds(width)

    def exchange(rows):
        return lax.all_to_all(rows, "hidden", split_axis=0, concat_axis=0, tiled=True)

    def down_send(lo, hi):
        return jnp.swapaxes(down_view[..., lo:hi], 0, 1)

    choice = jnp.concatenate([routes.astype(jnp.float32), route_weights], axis=1)
    tokens_all = lax.all_gather(tokens, "hidden", axis=0, tiled=True)
    choice_all = lax.all_gather(choice, "hidden", axis=0, tiled=True)
    cot_wide = cotangent.astype(jnp.float32)
    cot_sq = lax.all_gather(
        (cot_wide * cot_wide).astype(jnp.bfloat16), "hidden", axis=0, tiled=True
    )
    tok_count = tokens_all.shape[0]

    start_own = hidden_index * rows_dev + jnp.arange(local_count, dtype=jnp.int32) * slice_rows
    own_expert = (first_expert + start_own // F).astype(jnp.float32)
    named = choice_all[None, :, :top] == own_expert[:, None, None]
    weight_own = jnp.sum(jnp.where(named, choice_all[None, :, top:], 0.0), axis=2)
    dims = (((1,), (1,)), ((), ()))
    gate_value = lax.dot_general(
        gate_weight, tokens_all, dims, preferred_element_type=jnp.float32
    )
    up_value = lax.dot_general(up_weight, tokens_all, dims, preferred_element_type=jnp.float32)
    scaled = (jax.nn.silu(gate_value) * up_value).reshape(local_count, slice_rows, tok_count)
    scaled = scaled * weight_own[:, None, :]
    act = (scaled * scaled).astype(jnp.bfloat16)
    act = jnp.swapaxes(act.reshape(local_count, hidden_count, piece, tok_count), 0, 1)

    first = exchange(down_send(*bounds[0]))
    act, first = lax.optimization_barrier((act, first))
    act_units = exchange(act).reshape(units, piece, tok_count)

    sources = jnp.arange(hidden_count, dtype=jnp.int32)[:, None]
    local_ids = jnp.arange(local_count, dtype=jnp.int32)[None, :]
    start_row = (sources * rows_dev + local_ids * slice_rows).reshape(units)
    slot_table = slot_lookup(cluster, merged_slot)
    expert_ids = jnp.arange(EXPERTS, dtype=jnp.int32)
    unit_expert = first_expert + start_row // F
    unit_slot = jnp.sum(
        jnp.where(unit_expert[:, None] == expert_ids[None, :], slot_table[None, :], 0), axis=1
    )
    unit_slots = unit_slot * copies + start_row % F // slice_rows
    mixer = (
        unit_slots[None, :] == jnp.arange(slot_count, dtype=jnp.int32)[:, None]
    ).astype(jnp.bfloat16)

    act_part = jnp.einsum("su,uqt->sqt", mixer, act_units, preferred_element_type=jnp.float32)
    act_total = lax.psum_scatter(
        act_part.astype(jnp.bfloat16).reshape(MERGED, copies, piece, tok_count),
        "expert",
        scatter_dimension=0,
        tiled=True,
    )
    own_ids = expert_index * own_slots + jnp.arange(own_slots, dtype=jnp.int32)
    member_count = jnp.sum((slot_table[None, :] == own_ids[:, None]).astype(jnp.float32), axis=1)
    prior = PRIOR * member_count[:, None, None, None]

    merged = []
    numer_part, events = None, []
    for lo, hi in bounds:
        if numer_part is None:
            rows = first
        else:
            held = (down_send(lo, hi), numer_part, events[-2:-1])
            send, numer_part, _ = lax.optimization_barrier(held)
            rows = exchange(send)
        numer_part = fold(
            unit_slots,
            act_units,
            cot_sq[:, lo:hi],
            rows.reshape(units, piece, hi - lo),
            slot_count,
        )
        ready, _ = lax.optimization_barrier((numer_part, events[-1:]))
        numer_total = lax.psum_scatter(
            ready.reshape(MERGED, copies, piece, hi - lo),
            "expert",
            scatter_dimension=0,
            tiled=True,
        )
        events.append((numer_total, act_total))
        denom = jnp.einsum(
            "scqt,td->scqd", act_total, cot_sq[:, lo:hi], preferred_element_type=jnp.float32
        )
        merged.append((numer_total.astype(jnp.float32) / (denom + prior)).astype(jnp.bfloat16))
    return jnp.concatenate(merged, axis=3)


def solution(mesh):
    return jax.shard_map(
        per_device,
        mesh=mesh,
        in_specs=(
            P("hidden", None),
            P("hidden", None),
            P("hidden", None),
            P("hidden", None),
            P(("expert", "hidden"), None),
            P(("expert", "hidden"), None),
            P(("expert", "hidden"), None),
            P(),
            P(),
        ),
        out_specs=P("expert", None, "hidden", None),
        check_vma=False,
    )
```

time: 1120 us -> 603 us (0.54)
  waiting for transfers between devices: 569 us -> 130 us
  local copies, waits for them, and re-layouts: 113 us -> 36.7 us
  matrix products: 72.2 us -> 33 us
  blocking collectives: 322 us -> 345 us
  Pallas kernels: 0 us -> 22.1 us
    all_to_all x3, waiting for transfers between devices: 410 us -> 99.3 us  [exchange(): lax.all_to_all(rows, 'hidden', split_axis=0, concat_axis=0, tiled=True)]
    all_gather x0 -> x1, blocking collectives: none -> 153 us  [per_device(): choice_all = lax.all_gather(choice, 'hidden', axis=0, tiled=True)]
    reduce_scatter x2 -> x5, waiting for transfers between devices: 159 us -> 29.4 us  [the longest x4 29.4 us: per_device(): lax.psum_scatter(ready.reshape(MERGED, copies, piece, hi - lo), 'expert',...]
    all_to_all x1 -> x2, blocking collectives: 322 us -> 193 us  [exchange(): lax.all_to_all(rows, 'hidden', split_axis=0, concat_axis=0, tiled=True)]
    reshape x2 -> x1, local copies, waits for them, and re-layouts: 54.1 us -> 2.74 us  [per_device(): act_part.astype(jnp.bfloat16).reshape(MERGED, copies, piece, tok_count)]
    convert_element_type x2 -> x0, local copies, waits for them, and re-layouts: 46.5 us -> none  [the longest x1 23.2 us: per_device(): denom_part.astype(jnp.bfloat16)]
    dot_general x6 -> x7, matrix products: 72.2 us -> 33 us  [the longest x1 12 us: per_device(): lax.dot_general(gate_weight, tokens_all, dims, preferred_element_type=jnp...]
    pallas_call x0 -> x4, Pallas kernels: none -> 22.1 us  [fold(): pl.pallas_call(fold_kernel, grid_spec=pltpu.PrefetchScalarGridSpec(num_sc...]
  transfers between devices with their start and end apart: 5 -> 10, of which waited for: 4 -> 3; matrix products, arithmetic and copies ran while one was open for 7% -> 10% of each run, Pallas kernels for 0% -> 4%
where the time goes in v1:
time: 603 us
  blocking collectives  345 us (57%)
  waiting for transfers between devices  130 us (22%)
  local copies, waits for them, and re-layouts  36.7 us (6%)
  matrix products  33 us (5%)
  Pallas kernels  22.1 us (4%)
  starting transfers between devices  16.2 us (3%)
  between operations  13.8 us (2%)
  other arithmetic  6.3 us (1%)
    all_to_all x2, blocking collectives, exchange(): lax.all_to_all(rows, 'hidden', split_axis=0, concat_axis=0, tiled=True)  193 us
    all_gather x1, blocking collectives, per_device(): choice_all = lax.all_gather(choice, 'hidden', axis=0, tiled=True)  153 us
    all_to_all x3, waiting for transfers between devices, exchange(): lax.all_to_all(rows, 'hidden', split_axis=0, concat_axis=0, tiled=True)  99.3 us
    reduce_scatter x4, waiting for transfers between devices, per_device(): lax.psum_scatter(ready.reshape(MERGED, copies, piece, hi - lo), 'expert',...  29.4 us
    pallas_call x4, Pallas kernels, fold(): pl.pallas_call(fold_kernel, grid_spec=pltpu.PrefetchScalarGridSpec(num_sc...  22.1 us
    unnamed x38, local copies, waits for them, and re-layouts  18.6 us
    all_to_all x3, starting transfers between devices, exchange(): lax.all_to_all(rows, 'hidden', split_axis=0, concat_axis=0, tiled=True)  15.8 us
  transfers between devices with their start and end apart: 10, of which 3 were waited for; matrix products, arithmetic and copies ran while one was open for 10% of the time, Pallas kernels for 4%

profile of v1, /device:TPU:0, one launch (start us, length us, event | category | flops | bytes accessed | tf_op | source)
XLA Modules:
  0.0 602.8 jit_solution(7595094419226456421)
XLA Ops:
  7.3 7.7 %fusion.25 = (bf16[2,8,128,1024]{3,2,1,0:T(8,128)(2,1)}, bf16[2,8,128,1024]{3,2,1,0:T(8,128)(2,1)}, bf16[2,8,128,1024]{3,2,1,0:T(8,128)(2,1)S(1)}) fusion(bf16[2,8,128,3584]{3,2,1,0:T(8,128)(2,1)} %bitcast.90), kind=kLoop, calls=%fused_computation.64 | loop fusion | bytes 25165824 | tf_op jit(solution)/shard_map/slice | solution.py:101
  15.0 2.6 copy.74
  17.6 7.4 %all-to-all-start = ((bf16[8,2,128,1024]{3,2,1,0:T(8,128)(2,1)}), bf16[8,2,128,1024]{3,2,1,0:T(8,128)(2,1)}, u32[]{:S(2)}, u32[]{:S(2)}) async-start(bf16[8,2,128,1024]{3,2,1,0:T(8,128)(2,1)} %bitcast.87), calls=%async_computation | async-start | bytes 8388608 | tf_op jit(solution)/shard_map/all_to_all | solution.py:98
  25.9 152.5 %all-gather = f32[8,64,16]{1,2,0:T(8,128)S(1)} all-gather(f32[1,64,16]{1,2,0:T(8,128)S(1)} %maximum_bitcast_fusion.1), channel_id=1, replica_groups=mesh['expert'=4,'hidden'=8] {'hidden'}, dimensions={0}, use_global_device_ids=true | all-gather | bytes 36864 | tf_op jit(solution)/shard_map/all_gather | solution.py:105
  178.7 12.0 %fusion.28 = f32[2048,512]{1,0:T(8,128)S(1)} fusion(bf16[2048,3584]{1,0:T(8,128)(2,1)} %param.13, bf16[512,3584]{1,0:T(8,128)(2,1)} %all-gather.4.cloned.1.call-done), kind=kOutput, calls=%fused_computation.67 | convolution fusion | flops 7516192768 | bytes 22544384 | tf_op jit(solution)/shard_map/dot_general | solution.py:117
  190.7 11.1 %multiply_multiply_fusion = f32[2048,512]{1,0:T(8,128)S(1)} fusion(f32[2048,512]{1,0:T(8,128)S(1)} %fusion.28, bf16[2048,3584]{1,0:T(8,128)(2,1)} %param.14, bf16[512,3584]{1,0:T(8,128)(2,1)S(1)} %copy-done.10), kind=kOutput, calls=%fused_computation.7 | convolution fusion | flops 7521435648 | bytes 26738688 | tf_op jit(solution)/shard_map/dot_general | solution.py:120
  201.8 2.0 fusion.5
  203.9 4.0 all-to-all-start.1
  208.4 53.1 %all-to-all-done.1 = bf16[8,2,128,512]{3,2,1,0:T(8,128)(2,1)S(1)} async-done(((bf16[8,2,128,512]{3,2,1,0:T(8,128)(2,1)}), bf16[8,2,128,512]{3,2,1,0:T(8,128)(2,1)S(1)}, u32[]{:S(2)}, u32[]{:S(2)}) %all-to-all-start.1) | async-done | bytes 2097184 | tf_op jit(solution)/shard_map/all_to_all | solution.py:98
  261.6 1.5 convert_bitcast_fusion
  263.1 2.7 copy.50
  266.0 3.2 fusion.26
  269.1 6.8 %shard_map.91 = bf16[24,128,1024]{2,1,0:T(8,128)(2,1)S(1)} custom-call(s32[16]{0:T(128)S(1)} %fusion.19.slots_ref, bf16[16,128,512]{2,1,0:T(8,128)(2,1)S(1)} %bitcast.77, bf16[512,1024]{1,0:T(8,128)(2,1)S(1)} %get-tuple-element.24.cot_ref, bf16[16,128,1024]{2,1,0:T(8,128)(2,1)} %bitcast.6.down_ref), custom_call_target="tpu_custom_call" | custom-call | flops 2147483648 | bytes 10485760 | tf_op jit(solution)/shard_map/pallas_call | solution.py:44
  275.9 2.6 copy-done.2
  278.8 2.6 copy.73
  281.4 96.4 %all_to_all.25 = bf16[8,2,128,1024]{3,2,1,0:T(8,128)(2,1)S(1)} all-to-all(bf16[8,2,128,1024]{3,2,1,0:T(8,128)(2,1)S(1)} %bitcast.88), channel_id=1, replica_groups=mesh['expert'=4,'hidden'=8] {'hidden'}, dimensions={0} | all-to-all | bytes 8388608 | tf_op jit(solution)/shard_map/all_to_all | solution.py:98
  377.8 5.4 shard_map.92
  383.3 2.7 copy-done.1
  386.0 2.6 copy.72
  388.6 96.2 %all_to_all.26 = bf16[8,2,128,1024]{3,2,1,0:T(8,128)(2,1)S(1)} all-to-all(bf16[8,2,128,1024]{3,2,1,0:T(8,128)(2,1)S(1)} %bitcast.89), channel_id=1, replica_groups=mesh['expert'=4,'hidden'=8] {'hidden'}, dimensions={0} | all-to-all | bytes 8388608 | tf_op jit(solution)/shard_map/all_to_all | solution.py:98
  484.8 5.4 shard_map.93
  490.3 2.6 copy-done
  492.9 3.1 copy_bitcast_fusion.3
  496.0 4.4 all-to-all-start.4
  501.7 46.2 %all-to-all-done.4 = bf16[8,2,128,512]{3,2,1,0:T(8,128)(2,1)} async-done(((bf16[8,2,128,512]{3,2,1,0:T(8,128)(2,1)}), bf16[8,2,128,512]{3,2,1,0:T(8,128)(2,1)}, u32[]{:S(2)}, u32[]{:S(2)}) %all-to-all-start.4) | async-done | bytes 2097184 | tf_op jit(solution)/shard_map/all_to_all | solution.py:98
  547.9 4.4 shard_map.94
  552.3 1.7 copy-done.3
  554.2 2.9 fusion.4
  559.3 2.2 fusion.2
  561.5 29.4 %reduce-scatter.14.cloned.1.call-done = bf16[6,1,128,512]{3,2,0,1:T(8,128)(2,1)} async-done(((bf16[24,1,128,512]{3,2,0,1:T(8,128)(2,1)}), bf16[6,1,128,512]{3,2,0,1:T(8,128)(2,1)}) %reduce-scatter.14.cloned.1.call-update) | async-done | bytes 786448 | tf_op jit(solution)/shard_map/reduce_scatter | solution.py:172
  590.9 2.2 fusion.7
  593.2 2.7 maximum_bitcast_fusion
  (72 shorter events, 6.4 us)
Async XLA Ops:
  6.5 172.2 %all-gather.4.cloned.1.call-start = ((), (), s32[]{:S(2)}) async-start(), calls=%async_computation.10 | async-start | bytes 4128768 | tf_op jit(solution)/shard_map/all_gather | solution.py:104
  17.6 7.4 %copy-start.7 = (bf16[64,3584]{1,0:T(8,128)(2,1)S(1)}, bf16[64,3584]{1,0:T(8,128)(2,1)}, u32[]{:S(2)}) copy-start(bf16[64,3584]{1,0:T(8,128)(2,1)} %param.10) | copy-start | bytes 1376260
  17.6 8.3 %copy-start.8 = (s32[64,8]{0,1:T(8,128)S(1)}, s32[64,8]{0,1:T(8,128)}, u32[]{:S(2)}) copy-start(s32[64,8]{0,1:T(8,128)} %param.11) | copy-start | bytes 6148
  17.6 8.3 %copy-start.9 = (f32[64,8]{0,1:T(8,128)S(1)}, f32[64,8]{0,1:T(8,128)}, u32[]{:S(2)}) copy-start(f32[64,8]{0,1:T(8,128)} %param.12) | copy-start | bytes 6148
  17.6 186.3 %all-to-all-start = ((bf16[8,2,128,1024]{3,2,1,0:T(8,128)(2,1)}), bf16[8,2,128,1024]{3,2,1,0:T(8,128)(2,1)}, u32[]{:S(2)}, u32[]{:S(2)}) async-start(bf16[8,2,128,1024]{3,2,1,0:T(8,128)(2,1)} %bitcast.87), calls=%async_computation | async-start | bytes 8388608 | tf_op jit(solution)/shard_map/all_to_all | solution.py:98
  25.0 241.0 %all-gather.6.cloned.1.call-start = ((), (), s32[]{:S(2)}) async-start(), calls=%async_computation.11 | async-start | bytes 4128768 | tf_op jit(solution)/shard_map/all_gather | solution.py:107
  178.7 12.0 %copy-start.10 = (bf16[512,3584]{1,0:T(8,128)(2,1)S(1)}, bf16[512,3584]{1,0:T(8,128)(2,1)}, u32[]{:S(2)}) copy-start(bf16[512,3584]{1,0:T(8,128)(2,1)} %all-gather.4.cloned.1.call-done) | copy-start | bytes 11010052
  203.9 4.3 copy-start.15
  203.9 4.3 copy-start.16
  203.9 57.7 %all-to-all-start.1 = ((bf16[8,2,128,512]{3,2,1,0:T(8,128)(2,1)}), bf16[8,2,128,512]{3,2,1,0:T(8,128)(2,1)S(1)}, u32[]{:S(2)}, u32[]{:S(2)}) async-start(bf16[8,2,128,512]{3,2,1,0:T(8,128)(2,1)} %fusion.5), calls=%async_computation.1 | async-start | bytes 4194304 | tf_op jit(solution)/shard_map/all_to_all | solution.py:98
  207.9 178.0 %reduce-scatter.8.cloned.1.call-start = ((), (), s32[]{:S(2)}) async-start(), calls=%async_computation.13 | async-start | bytes 3932160 | tf_op jit(solution)/shard_map/reduce_scatter | solution.py:145
  265.9 120.0 %reduce-scatter.6.cloned.1.call-start = ((), (), s32[]{:S(2)}) async-start(), calls=%async_computation.12 | async-start | bytes 7864320 | tf_op jit(solution)/shard_map/reduce_scatter | solution.py:172
  275.9 2.6 copy-start.2
  278.6 214.3 %reduce-scatter.10.cloned.1.call-start = ((), (), s32[]{:S(2)}) async-start(), calls=%async_computation.14 | async-start | bytes 7864320 | tf_op jit(solution)/shard_map/reduce_scatter | solution.py:172
  281.4 96.4 %copy-start.4 = (bf16[512,1024]{1,0:T(8,128)(2,1)S(1)}, bf16[512,1024]{1,0:T(8,128)(2,1)}, u32[]{:S(2)}) copy-start(bf16[512,1024]{1,0:T(8,128)(2,1)} %get-tuple-element.26.cot_ref) | copy-start | bytes 3145732
  383.2 2.7 copy-start.1
  385.9 168.0 %reduce-scatter.12.cloned.1.call-start = ((), (), s32[]{:S(2)}) async-start(), calls=%async_computation.15 | async-start | bytes 7864320 | tf_op jit(solution)/shard_map/reduce_scatter | solution.py:172
  490.3 2.6 copy-start
  496.0 51.8 %all-to-all-start.4 = ((bf16[8,2,128,512]{3,2,1,0:T(8,128)(2,1)}), bf16[8,2,128,512]{3,2,1,0:T(8,128)(2,1)}, u32[]{:S(2)}, u32[]{:S(2)}) async-start(bf16[8,2,128,512]{3,2,1,0:T(8,128)(2,1)} %copy_bitcast_fusion.3), calls=%async_computation.8 | async-start | bytes 4194304 | tf_op jit(solution)/shard_map/all_to_all | solution.py:98
  500.4 90.5 %reduce-scatter.14.cloned.1.call-start = ((), (), s32[]{:S(2)}) async-start(), calls=%async_computation.16 | async-start | bytes 3932160 | tf_op jit(solution)/shard_map/reduce_scatter | solution.py:172
  547.9 6.3 %copy-start.13 = (bf16[6,1,128,512]{3,2,1,0:T(8,128)(2,1)S(1)}, bf16[6,1,128,512]{3,2,1,0:T(8,128)(2,1)}, u32[]{:S(2)}) copy-start(bf16[6,1,128,512]{3,2,1,0:T(8,128)(2,1)} %reduce-scatter.8.cloned.1.call-done) | copy-start | bytes 2359300
  552.3 1.7 copy-start.3
  554.2 3.0 copy-start.5
  554.2 3.3 copy-start.11
  554.2 3.5 copy-start.14
  557.7 1.7 copy-start.12
  590.9 2.3 copy-start.6
Sparse Core Ops, SparseCore 0:
  9.5 142.8 all-gather.3
  154.6 72.7 all-gather.5
  266.0 36.5 reduce-scatter.7
  305.2 58.3 reduce-scatter.5
  386.1 57.0 reduce-scatter.9
  493.1 57.0 reduce-scatter.11
  554.1 36.7 reduce-scatter.13
